TPU v7x, 256 devices: a whole 4x4x8 slice. The times are simulated.
256 devices in a mesh: ctx: 32 (over z, x), tp: 8 (over y, core).
Axes of the slice: x: 4, y: 4, z: 8, core: 2. Of those that a mesh axis runs over, the one named last changes fastest.
Arguments:
- query_in: bfloat16 [16384, 8192], P('ctx', 'tp'), may hold values from -6 to 6
- key_in: bfloat16 [16384, 8192], P('ctx', 'tp'), may hold values from -6 to 6
- value_in: bfloat16 [16384, 8192], P('ctx', 'tp'), may hold values from -6 to 6
- filters: bfloat16 [512, 128], P('tp'), may hold values from -0.5 to 0.5
- proj_out: bfloat16 [4096, 8192], P('ctx', 'tp'), may hold values from -0.0625 to 0.0625
- cotangent: bfloat16 [16384, 4096], P('ctx', 'tp'), may hold values from -6 to 6
Outputs:
- grad_query: bfloat16 [16384, 8192], P('ctx', 'tp')
- grad_key: bfloat16 [16384, 8192], P('ctx', 'tp')
- grad_value: bfloat16 [16384, 8192], P('ctx', 'tp')
- grad_filter: float32 [512, 128], P('tp')
- grad_proj: float32 [4096, 8192], P('ctx', 'tp')
All inputs are finite; a program needn't handle non-finite values.
Results may differ from a plain program's by a relative error of at most 0.005.
Values may be sent and summed in bfloat16 or wider, within the bound.
No kernel may reach another device: no remote copies, remote signals or barrier semaphores. Data moves between devices by JAX's collectives and lax.ppermute only.
A program may use at most 192 MiB of HBM per device.

v0:
```python
import jax
import jax.numpy as jnp
from jax import lax
from jax.sharding import PartitionSpec as P


def from_behind(value, axis, by):
    count = lax.axis_size(axis)
    pairs = [(i, i + by) for i in range(count) if 0 <= i + by < count]
    return lax.ppermute(value, axis, pairs)


def toeplitz_rows(filters):
    group_count, tap_count = filters.shape
    padded = jnp.concatenate(
        [
            jnp.zeros((group_count, 1), filters.dtype),
            jnp.flip(filters, 1),
            jnp.zeros((group_count, 2 * tap_count - 1), filters.dtype),
        ],
        1,
    )
    tiled = jnp.tile(padded, (1, tap_count))[:, : tap_count * (3 * tap_count - 1)]
    return tiled.reshape(group_count, tap_count, 3 * tap_count - 1)[:, :, : 2 * tap_count]


def on_device(query_in, key_in, value_in, filters, proj_out, cotangent):
    tok_rows, chan_width = query_in.shape
    group_count, tap_count = filters.shape
    group_size = chan_width // group_count
    blocks = tok_rows // tap_count
    table = toeplitz_rows(filters)
    mixed_in = (key_in.astype(jnp.float32) * value_in.astype(jnp.float32)).astype(jnp.bfloat16)
    left_rim = from_behind(mixed_in[tok_rows - tap_count + 1 :], "ctx", 1)
    extended = jnp.concatenate(
        [jnp.zeros((1, chan_width), jnp.bfloat16), left_rim, mixed_in[: tok_rows - tap_count]], 0
    )
    window = jnp.concatenate(
        [
            extended.reshape(blocks, tap_count, group_count, group_size),
            mixed_in.reshape(blocks, tap_count, group_count, group_size),
        ],
        1,
    )
    conv_out = jnp.einsum(
        "gts,bsgc->btgc", table, window, preferred_element_type=jnp.float32
    ).reshape(tok_rows, chan_width)
    gated = (query_in.astype(jnp.float32) * conv_out).astype(jnp.bfloat16)
    cot_full = lax.all_gather(cotangent, "tp", axis=1, tiled=True)
    columns = cot_full
    grad_all = jnp.dot(
        columns,
        lax.all_gather(proj_out, "ctx", axis=0, tiled=True),
        preferred_element_type=jnp.float32,
    )
    grad_query = (grad_all * conv_out).astype(jnp.bfloat16)
    grad_inner = (grad_all * query_in.astype(jnp.float32)).astype(jnp.bfloat16)
    next_rows = from_behind(grad_inner[: tap_count - 1], "ctx", -1)
    ahead = jnp.concatenate(
        [grad_inner[tap_count:], next_rows, jnp.zeros((1, chan_width), jnp.bfloat16)], 0
    )
    inner_blocks = grad_inner.reshape(blocks, tap_count, group_count, group_size)
    ahead_blocks = ahead.reshape(blocks, tap_count, group_count, group_size)
    grad_mixed = jnp.einsum(
        "gts,btgc->bsgc", table[:, :, tap_count:], inner_blocks, preferred_element_type=jnp.float32
    )
    grad_mixed = grad_mixed + jnp.einsum(
        "gts,btgc->bsgc", table[:, :, :tap_count], ahead_blocks, preferred_element_type=jnp.float32
    )
    grad_mixed = grad_mixed.reshape(tok_rows, chan_width)
    grad_key = (grad_mixed * value_in.astype(jnp.float32)).astype(jnp.bfloat16)
    grad_value = (grad_mixed * key_in.astype(jnp.float32)).astype(jnp.bfloat16)
    corr = jnp.einsum("btgc,bsgc->gts", inner_blocks, window, preferred_element_type=jnp.float32)
    skewed = jnp.pad(corr.reshape(group_count, -1), ((0, 0), (0, tap_count))).reshape(
        group_count, tap_count, 2 * tap_count + 1
    )
    filter_part = jnp.flip(jnp.sum(skewed, axis=1)[:, 1 : tap_count + 1], 1)
    columns = cot_full
    grad_proj = lax.psum_scatter(
        lax.dot_general(
            columns, gated, (((0,), (0,)), ((), ())), preferred_element_type=jnp.float32
        ),
        "ctx",
        scatter_dimension=0,
        tiled=True,
    )
    grad_filter = lax.psum(filter_part, "ctx")
    return (grad_query, grad_key, grad_value, grad_filter, grad_proj)


def solution(mesh):
    placed = (
        P("ctx", "tp"),
        P("ctx", "tp"),
        P("ctx", "tp"),
        P("tp", None),
        P("ctx", "tp"),
        P("ctx", "tp"),
    )
    return jax.shard_map(
        on_device,
        mesh=mesh,
        in_specs=placed,
        out_specs=(P("ctx", "tp"), P("ctx", "tp"), P("ctx", "tp"), P("tp", None), P("ctx", "tp")),
        check_vma=False,
    )
```

profile of v0, /device:TPU:8, one launch (start us, length us, event | category | flops | bytes accessed | tf_op | source)
XLA Modules:
  0.0 496.2 jit_solution(13362791816464786184)
XLA Ops:
  7.2 0.7 all-gather.3.cloned.1.call-update
  7.9 0.7 all-gather.5.cloned.1.call-update
  8.7 37.7 %all-gather.3.cloned.1.call-done = bf16[512,4096]{1,0:T(8,128)(2,1)} async-done(((bf16[512,512]{1,0:T(8,128)(2,1)}), bf16[512,4096]{1,0:T(8,128)(2,1)}) %all-gather.3.cloned.1.call-update) | async-done | bytes 4194320 | tf_op jit(solution)/shard_map/all_gather | solution.py:49
  46.4 101.9 %all-gather.5.cloned.1.call-done = bf16[4096,1024]{1,0:T(8,128)(2,1)} async-done(((bf16[128,1024]{1,0:T(8,128)(2,1)}), bf16[4096,1024]{1,0:T(8,128)(2,1)}) %all-gather.5.cloned.1.call-update) | async-done | bytes 8388624 | tf_op jit(solution)/shard_map/all_gather | solution.py:53
  148.3 10.6 %fusion.4 = (bf16[512,1024]{1,0:T(8,128)(2,1)S(1)}, f32[512,1024]{1,0:T(8,128)}) fusion(bf16[512,1024]{1,0:T(8,128)(2,1)} %param.6, bf16[512,4096]{1,0:T(8,128)(2,1)} %all-gather.3.cloned.1.call-done, bf16[4096,1024]{1,0:T(8,128)(2,1)} %all-gather.5.cloned.1.call-done), kind=kOutput, calls=%fused_computation.11 | convolution fusion | flops 4296540160 | bytes 16777216 | tf_op jit(solution)/shard_map/dot_general | solution.py:51
  159.0 1.5 collective-permute-start.1
  160.7 0.5 copy.16
  161.2 2.3 copy.17
  163.6 0.5 tile.4
  164.2 4.1 copy.37
  168.2 3.1 slice.40
  171.3 16.4 %reshape.43 = bf16[64,128,383]{2,1,0:T(8,128)(2,1)} reshape(bf16[64,49024]{1,0:T(8,128)(2,1)} %slice.40) | data formatting | bytes 12550144 | tf_op jit(solution)/shard_map/reshape | solution.py:24
  187.7 0.9 slice.43
  188.7 1.3 copy.23
  190.0 1.3 reshape.45
  191.3 1.5 maximum_maximum_fusion
  192.8 1.3 copy.25
  194.1 1.3 reshape.46
  195.5 2.3 fusion.6
  197.7 2.3 add_bitcast_fusion
  200.1 1.0 copy.27
  201.0 0.2 copy-done.1
  201.3 2.0 fusion.1
  203.2 0.1 slice.38
  203.4 5.3 %collective-permute-start = (bf16[127,1024]{0,1:T(8,128)(2,1)S(1)}, bf16[127,1024]{0,1:T(8,128)(2,1)}, u32[]{:S(2)}, u32[]{:S(2)}) collective-permute-start(bf16[127,1024]{0,1:T(8,128)(2,1)S(1)} %slice.38), channel_id=1, source_target_pairs={{0,8},{8,16},{16,24},{24,32},{32,40},{40,48},{48,56},{56,64},{64,7... | collective-permute-start | bytes 780296 | tf_op jit(solution)/shard_map/ppermute | solution.py:10
  208.7 1.0 slice.39
  209.6 0.3 reshape.42
  209.9 2.9 collective-permute-done
  212.8 2.5 pad_maximum_fusion
  215.3 1.3 reshape.41
  216.6 0.3 copy_dynamic-update-slice_fusion.1
  216.9 0.4 copy_dynamic-update-slice_fusion
  217.3 4.5 fusion.8
  221.9 1.0 copy.21
  222.8 1.5 copy.52
  224.4 1.9 copy.22
  226.3 12.8 %convolution_bitcast_fusion = f32[4096,1024]{0,1:T(8,128)} fusion(bf16[512,4096]{1,0:T(8,128)(2,1)} %all-gather.3.cloned.1.call-done, f32[512,1024]{1,0:T(8,128)S(1)} %copy.22, bf16[512,1024]{1,0:T(8,128)(2,1)} %param.6), kind=kOutput, calls=%fused_computation | convolution fusion | flops 4296540160 | bytes 24117248 | tf_op jit(solution)/shard_map/dot_general | solution.py:80
  239.1 2.3 copy.31
  241.4 2.3 copy.30
  243.7 2.9 fusion.11
  246.6 4.7 copy.40
  251.3 3.9 pad.4
  255.2 14.2 %reshape.49 = f32[64,128,257]{2,1,0:T(8,128)} reshape(f32[64,32896]{1,0:T(8,128)} %pad.4) | data formatting | bytes 16842752 | tf_op jit(solution)/shard_map/reshape | solution.py:74
  269.4 6.2 %reduce_sum.9 = f32[64,257]{1,0:T(8,128)S(1)} reduce(f32[64,128,257]{2,1,0:T(8,128)} %reshape.49, f32[]{:T(128)} %constant.3.clone.1), dimensions={1}, to_apply=%region_0.1 | reduce | flops 2088896 | bytes 8487172 | tf_op jit(solution)/shard_map/reduce_sum | solution.py:77
  275.8 143.0 %psum.7 = f32[64,128]{1,0:T(8,128)} all-reduce(f32[64,128]{1,0:T(8,128)S(1)} %rev.9), channel_id=1, replica_groups=mesh['ctx'=32,'tp'=8] {'ctx'}, use_global_device_ids=true, to_apply=%region_1.2 | all-reduce | flops 8192 | bytes 65536 | tf_op jit(solution)/shard_map/psum | solution.py:87
  418.7 2.9 multiply_convert_fusion
  421.6 66.0 %reduce-scatter.2.cloned.1.call-done = f32[128,1024]{0,1:T(8,128)} async-done(((f32[4096,1024]{0,1:T(8,128)}), f32[128,1024]{0,1:T(8,128)}) %reduce-scatter.2.cloned.1.call-update) | async-done | bytes 524304 | tf_op jit(solution)/shard_map/reduce_scatter | solution.py:79
  487.7 2.0 copy.32
  (22 shorter events, 0.7 us)
Async XLA Ops:
  7.2 39.2 %all-gather.3.cloned.1.call-start = ((), (), s32[]{:S(2)}) async-start(), calls=%async_computation.1 | async-start | bytes 4718592 | tf_op jit(solution)/shard_map/all_gather | solution.py:49
  7.9 140.4 %all-gather.5.cloned.1.call-start = ((), (), s32[]{:S(2)}) async-start(), calls=%async_computation.2 | async-start | bytes 8650752 | tf_op jit(solution)/shard_map/all_gather | solution.py:53
  8.6 152.0 %copy-start.3 = (bf16[64,128]{1,0:T(8,128)(2,1)S(1)}, bf16[64,128]{1,0:T(8,128)(2,1)}, u32[]{:S(2)}) copy-start(bf16[64,128]{1,0:T(8,128)(2,1)} %param.9) | copy-start | bytes 49156
  8.7 152.0 %copy-start.2 = (bf16[512,1024]{1,0:T(8,128)(2,1)S(1)}, bf16[512,1024]{1,0:T(8,128)(2,1)}, u32[]{:S(2)}) copy-start(bf16[512,1024]{1,0:T(8,128)(2,1)} %param.7) | copy-start | bytes 3145732
  8.7 479.0 %reduce-scatter.2.cloned.1.call-start = ((), (), s32[]{:S(2)}) async-start(), calls=%async_computation.3 | async-start | bytes 17301504 | tf_op jit(solution)/shard_map/reduce_scatter | solution.py:79
  159.0 32.4 %collective-permute-start.1 = (bf16[127,1024]{1,0:T(8,128)(2,1)S(1)}, bf16[127,1024]{1,0:T(8,128)(2,1)}, u32[]{:S(2)}, u32[]{:S(2)}) collective-permute-start(bf16[127,1024]{1,0:T(8,128)(2,1)S(1)} %slice.44), channel_id=1, source_target_pairs={{8,0},{16,8},{24,16},{32,24},{40,32},{48,40},{56,48},{64,56},{72,6... | collective-permute-start | bytes 780296 | tf_op jit(solution)/shard_map/ppermute | solution.py:10
  200.0 1.2 copy-start.1
  203.4 9.4 %collective-permute-start = (bf16[127,1024]{0,1:T(8,128)(2,1)S(1)}, bf16[127,1024]{0,1:T(8,128)(2,1)}, u32[]{:S(2)}, u32[]{:S(2)}) collective-permute-start(bf16[127,1024]{0,1:T(8,128)(2,1)S(1)} %slice.38), channel_id=1, source_target_pairs={{0,8},{8,16},{16,24},{24,32},{32,40},{40,48},{48,56},{56,64},{64,7... | collective-permute-start | bytes 780296 | tf_op jit(solution)/shard_map/ppermute | solution.py:10
  217.3 4.5 copy-start
Sparse Core Ops, SparseCore 0:
  9.8 36.5 all-gather.2
  49.0 99.3 all-gather.4
  239.3 248.3 reduce-scatter.1
where the time goes:
time: 497 us; the launch traced here: 496 us
  waiting for transfers between devices  210 us (42%)
  blocking collectives  143 us (29%)
  local copies, waits for them, and re-layouts  72 us (14%)
  matrix products  35.4 us (7%)
  other arithmetic  15.1 us (3%)
  between operations  14 us (3%)
  starting transfers between devices  6.87 us (1%)
    psum x1, blocking collectives, on_device(): grad_filter = lax.psum(filter_part, 'ctx')  143 us
    all_gather x1, waiting for transfers between devices, on_device(): lax.all_gather(proj_out, 'ctx', axis=0, tiled=True)  102 us
    reduce_scatter x1, waiting for transfers between devices, on_device(): lax.psum_scatter(lax.dot_general(columns, gated, (((0,), (0,)), ((), ()))...  66 us
    all_gather x1, waiting for transfers between devices, on_device(): cot_full = lax.all_gather(cotangent, 'tp', axis=1, tiled=True)  37.7 us
    unnamed x17, local copies, waits for them, and re-layouts  20.2 us
    reshape x1, local copies, waits for them, and re-layouts, toeplitz_rows(): tiled.reshape(group_count, tap_count, 3 * tap_count - 1)  16.4 us
    reshape x1, local copies, waits for them, and re-layouts, on_device(): jnp.pad(corr.reshape(group_count, -1), ((0, 0), (0, tap_count)))  14.2 us
    dot_general x1, matrix products, on_device(): lax.dot_general(columns, gated, (((0,), (0,)), ((), ())), preferred_eleme...  12.8 us
  transfers between devices with their start and end apart: 5, of which 4 were waited for; matrix products, arithmetic and copies ran while one was open for 14% of the time, Pallas kernels for 0%

commit v1 on v0

--- a/solution.py
+++ b/solution.py
@@ -84,7 +84,7 @@
         scatter_dimension=0,
         tiled=True,
     )
-    grad_filter = lax.psum(filter_part, "ctx")
+    grad_filter = jnp.sum(lax.all_gather(filter_part, "ctx"), axis=0)
     return (grad_query, grad_key, grad_value, grad_filter, grad_proj)
 
 

time: 497 us -> 582 us (1.17)
  waiting for transfers between devices: 210 us -> 443 us
  blocking collectives: 143 us -> 0 us
    reduce_scatter x1, waiting for transfers between devices: 66 us -> 245 us  [on_device(): lax.psum_scatter(lax.dot_general(columns, gated, (((0,), (0,)), ((), ()))...]
    psum x1 -> x0, blocking collectives: 143 us -> none  [on_device(): grad_filter = lax.psum(filter_part, 'ctx')]
    all_gather x0 -> x1, waiting for transfers between devices: none -> 53.6 us  [on_device(): grad_filter = jnp.sum(lax.all_gather(filter_part, 'ctx'), axis=0)]
    unnamed x17 -> x21, local copies, waits for them, and re-layouts: 20.2 us -> 20.7 us
  transfers between devices with their start and end apart: 5 -> 6, of which waited for: 4 -> 5; matrix products, arithmetic and copies ran while one was open for 14% -> 10% of each run, Pallas kernels for 0% -> 0%
where the time goes in v1:
time: 582 us; the launch traced here: 581 us
  waiting for transfers between devices  443 us (76%)
  local copies, waits for them, and re-layouts  72.8 us (13%)
  matrix products  30.6 us (5%)
  other arithmetic  14.7 us (3%)
  between operations  14 us (2%)
  starting transfers between devices  6.67 us (1%)
    reduce_scatter x1, waiting for transfers between devices, on_device(): lax.psum_scatter(lax.dot_general(columns, gated, (((0,), (0,)), ((), ()))...  245 us
    all_gather x1, waiting for transfers between devices, on_device(): lax.all_gather(proj_out, 'ctx', axis=0, tiled=True)  102 us
    all_gather x1, waiting for transfers between devices, on_device(): grad_filter = jnp.sum(lax.all_gather(filter_part, 'ctx'), axis=0)  53.6 us
    all_gather x1, waiting for transfers between devices, on_device(): cot_full = lax.all_gather(cotangent, 'tp', axis=1, tiled=True)  37.7 us
    unnamed x21, local copies, waits for them, and re-layouts  20.7 us
    reshape x1, local copies, waits for them, and re-layouts, toeplitz_rows(): tiled.reshape(group_count, tap_count, 3 * tap_count - 1)  16.4 us
    reshape x1, local copies, waits for them, and re-layouts, on_device(): jnp.pad(corr.reshape(group_count, -1), ((0, 0), (0, tap_count)))  14.2 us
  transfers between devices with their start and end apart: 6, of which 5 were waited for; matrix products, arithmetic and copies ran while one was open for 10% of the time, Pallas kernels for 0%

profile of v1, /device:TPU:8, one launch (start us, length us, event | category | flops | bytes accessed | tf_op | source)
XLA Modules:
  0.0 581.5 jit_solution(3688133445575276091)
XLA Ops:
  7.2 0.7 all-gather.5.cloned.1.call-update
  7.9 0.7 all-gather.7.cloned.1.call-update
  8.7 37.7 %all-gather.5.cloned.1.call-done = bf16[512,4096]{1,0:T(8,128)(2,1)} async-done(((bf16[512,512]{1,0:T(8,128)(2,1)}), bf16[512,4096]{1,0:T(8,128)(2,1)}) %all-gather.5.cloned.1.call-update) | async-done | bytes 4194320 | tf_op jit(solution)/shard_map/all_gather | solution.py:49
  46.4 101.9 %all-gather.7.cloned.1.call-done = bf16[4096,1024]{1,0:T(8,128)(2,1)} async-done(((bf16[128,1024]{1,0:T(8,128)(2,1)}), bf16[4096,1024]{1,0:T(8,128)(2,1)}) %all-gather.7.cloned.1.call-update) | async-done | bytes 8388624 | tf_op jit(solution)/shard_map/all_gather | solution.py:53
  148.3 10.6 %fusion.4 = (bf16[512,1024]{1,0:T(8,128)(2,1)S(1)}, f32[512,1024]{1,0:T(8,128)}) fusion(bf16[512,1024]{1,0:T(8,128)(2,1)} %param.6, bf16[512,4096]{1,0:T(8,128)(2,1)} %all-gather.5.cloned.1.call-done, bf16[4096,1024]{1,0:T(8,128)(2,1)} %all-gather.7.cloned.1.call-done), kind=kOutput, calls=%fused_computation.11 | convolution fusion | flops 4296540160 | bytes 16777216 | tf_op jit(solution)/shard_map/dot_general | solution.py:51
  158.9 1.5 collective-permute-start.1
  160.7 0.5 copy.33
  161.2 2.3 copy.34
  163.6 0.5 tile.4
  164.2 4.1 copy.54
  168.2 3.1 slice.40
  171.3 16.4 %reshape.43 = bf16[64,128,383]{2,1,0:T(8,128)(2,1)} reshape(bf16[64,49024]{1,0:T(8,128)(2,1)} %slice.40) | data formatting | bytes 12550144 | tf_op jit(solution)/shard_map/reshape | solution.py:24
  187.7 0.9 slice.43
  188.7 1.3 copy.40
  190.0 1.3 reshape.45
  191.3 1.5 maximum_maximum_fusion
  192.8 1.3 copy.42
  194.1 1.3 reshape.46
  195.5 2.3 fusion.6
  197.7 2.3 add_bitcast_fusion
  200.1 1.0 copy.44
  201.3 2.0 fusion.1
  203.4 4.8 collective-permute-start
  208.3 1.1 reshape.42
  209.4 3.4 collective-permute-done
  212.8 0.3 pad_maximum_fusion
  213.1 1.1 reshape.41
  214.2 1.6 copy_dynamic-update-slice_fusion.1
  215.9 0.4 copy_dynamic-update-slice_fusion
  216.3 1.3 fusion.11
  217.6 4.7 copy.57
  222.3 3.8 pad.4
  226.1 14.2 %reshape.49 = f32[64,128,257]{2,1,0:T(8,128)} reshape(f32[64,32896]{1,0:T(8,128)} %pad.4) | data formatting | bytes 16842752 | tf_op jit(solution)/shard_map/reshape | solution.py:74
  240.3 6.1 %reduce_sum.18 = f32[64,257]{1,0:T(8,128)S(1)} reduce(f32[64,128,257]{2,1,0:T(8,128)} %reshape.49, f32[]{:T(128)} %constant.3.clone.1), dimensions={1}, to_apply=%region_0.1 | reduce | flops 2088896 | bytes 8487172 | tf_op jit(solution)/shard_map/reduce_sum | solution.py:77
  246.4 0.7 rev.9
  247.2 0.3 reduce-scatter.2.cloned.1.call-start
  247.5 3.7 fusion.8
  251.2 1.0 copy.38
  252.2 1.5 copy.69
  253.7 2.0 copy.39
  255.7 10.4 %convolution_bitcast_fusion = f32[4096,1024]{0,1:T(8,128)} fusion(bf16[512,4096]{1,0:T(8,128)(2,1)} %all-gather.5.cloned.1.call-done, f32[512,1024]{1,0:T(8,128)S(1)} %copy.39, bf16[512,1024]{1,0:T(8,128)(2,1)S(1)} %copy-done.3), kind=kOutput, calls=%fused_computation | convolution fusion | flops 4296540160 | bytes 24117248 | tf_op jit(solution)/shard_map/dot_general | solution.py:80
  266.1 2.4 copy.48
  268.5 1.3 copy.47
  269.8 2.9 multiply_convert_fusion
  272.6 53.6 %all-gather.9.cloned.1.call-done = f32[2048,128]{1,0:T(8,128)} async-done(((f32[64,128]{1,0:T(8,128)}), f32[2048,128]{1,0:T(8,128)}) %all-gather.9.cloned.1.call-update) | async-done | bytes 1048592 | tf_op jit(solution)/shard_map/all_gather | solution.py:87
  326.3 1.9 reduce_sum.19
  328.2 244.7 %reduce-scatter.2.cloned.1.call-done = f32[128,1024]{0,1:T(8,128)} async-done(((f32[4096,1024]{0,1:T(8,128)}), f32[128,1024]{0,1:T(8,128)}) %reduce-scatter.2.cloned.1.call-update) | async-done | bytes 524304 | tf_op jit(solution)/shard_map/reduce_scatter | solution.py:79
  572.9 2.0 copy.49
  (29 shorter events, 1.1 us)
Async XLA Ops:
  7.2 39.2 %all-gather.5.cloned.1.call-start = ((), (), s32[]{:S(2)}) async-start(), calls=%async_computation.1 | async-start | bytes 4718592 | tf_op jit(solution)/shard_map/all_gather | solution.py:49
  7.9 140.4 %all-gather.7.cloned.1.call-start = ((), (), s32[]{:S(2)}) async-start(), calls=%async_computation.2 | async-start | bytes 8650752 | tf_op jit(solution)/shard_map/all_gather | solution.py:53
  8.6 151.9 %copy-start.5 = (bf16[64,128]{1,0:T(8,128)(2,1)S(1)}, bf16[64,128]{1,0:T(8,128)(2,1)}, u32[]{:S(2)}) copy-start(bf16[64,128]{1,0:T(8,128)(2,1)} %param.9) | copy-start | bytes 49156
  8.7 152.0 %copy-start.4 = (bf16[512,1024]{1,0:T(8,128)(2,1)S(1)}, bf16[512,1024]{1,0:T(8,128)(2,1)}, u32[]{:S(2)}) copy-start(bf16[512,1024]{1,0:T(8,128)(2,1)} %param.7) | copy-start | bytes 3145732
  8.7 317.6 %all-gather.9.cloned.1.call-start = ((), (), s32[]{:S(2)}) async-start(), calls=%async_computation.4 | async-start | bytes 1081344 | tf_op jit(solution)/shard_map/all_gather | solution.py:87
  158.9 32.4 %collective-permute-start.1 = (bf16[127,1024]{1,0:T(8,128)(2,1)S(1)}, bf16[127,1024]{1,0:T(8,128)(2,1)}, u32[]{:S(2)}, u32[]{:S(2)}) collective-permute-start(bf16[127,1024]{1,0:T(8,128)(2,1)S(1)} %slice.44), channel_id=1, source_target_pairs={{8,0},{16,8},{24,16},{32,24},{40,32},{48,40},{56,48},{64,56},{72,6... | collective-permute-start | bytes 780296 | tf_op jit(solution)/shard_map/ppermute | solution.py:10
  200.0 1.2 copy-start.1
  203.4 9.4 %collective-permute-start = (bf16[127,1024]{0,1:T(8,128)(2,1)S(1)}, bf16[127,1024]{0,1:T(8,128)(2,1)S(1)}, u32[]{:S(2)}, u32[]{:S(2)}) collective-permute-start(bf16[127,1024]{0,1:T(8,128)(2,1)S(1)} %slice.38), channel_id=1, source_target_pairs={{0,8},{8,16},{16,24},{24,32},{32,40},{40,48},{48,56},{56,64},{64,7... | collective-permute-start | bytes 780296 | tf_op jit(solution)/shard_map/ppermute | solution.py:10
  214.2 1.6 copy-start.2
  247.2 325.7 %reduce-scatter.2.cloned.1.call-start = ((), (), s32[]{:S(2)}) async-start(), calls=%async_computation.3 | async-start | bytes 17301504 | tf_op jit(solution)/shard_map/reduce_scatter | solution.py:79
  253.7 2.0 copy-start.3
  266.1 2.4 copy-start
Sparse Core Ops, SparseCore 0:
  9.8 36.5 all-gather.4
  49.0 99.3 all-gather.6
  247.3 78.9 all-gather.8
  330.3 242.6 reduce-scatter.1
